TPU v7x, 32 devices: a whole 2x2x4 slice. The times are simulated.
32 devices in a mesh: ang: 4 (over x, core), row: 8 (over z, y).
Axes of the slice: x: 2, y: 2, z: 4, core: 2. Of those that a mesh axis runs over, the one named last changes fastest.
Arguments:
- patches: bfloat16 [384, 2, 256, 256], P(('ang', 'row')), may hold values from -6 to 6
- owner: int32 [384], P(('ang', 'row')), may hold values from 0 to 7, as said below
- column: int32 [384], P(('ang', 'row')), may hold values from 0 to 1792
- angle_slot: int32 [384], P(('ang', 'row')), may hold values from 0 to 1
- probe: bfloat16 [2, 256, 256], replicated, may hold values from -1 to 1
- frames: bfloat16 [512, 256, 256], P(('ang', 'row')), may hold values from 0.099609375 to 3
- projection: bfloat16 [8, 2048, 2048], P('ang', 'row'), may hold values from -6 to 6
Outputs:
- refined_patches: bfloat16 [384, 2, 256, 256], P(('ang', 'row'))
- sinogram: bfloat16 [8, 8, 256, 2048], P(None, 'row', 'ang')
Inputs may be any that keep to these rules, and one draw needn't show every extreme that they name: Among one device's 12 positions no owner appears more than 2 times; in every angle group one owner band receives exactly 2 positions from every device of the group.
All inputs are finite; a program needn't handle non-finite values.
Results may differ from a plain program's by a relative error of at most 0.0059.
Values may be sent and summed in bfloat16 or wider, within the bound.
A program may use at most 128 MiB of HBM per device.

v0:
```python
import math

import jax
import jax.numpy as jnp
from jax import lax
from jax.sharding import PartitionSpec as P


def dft_tables(size):
    positions = jnp.arange(size, dtype=jnp.int32)
    product = positions[:, None] * positions[None, :] % size
    phase = product.astype(jnp.float32) * (2.0 * math.pi / size)
    factor = 1.0 / math.sqrt(size)
    return (
        (jnp.cos(phase) * factor).astype(jnp.bfloat16),
        (-jnp.sin(phase) * factor).astype(jnp.bfloat16),
    )


def left_product(table, stacked):
    return jnp.einsum("ij,njk->nik", table, stacked, preferred_element_type=jnp.float32)


def right_product(stacked, table):
    return jnp.einsum("nij,jk->nik", stacked, table, preferred_element_type=jnp.float32)


def refine_batch(objects, frame_stack, probe, real_table, imag_table, scale_den):
    probe_real = probe[0].astype(jnp.float32)
    probe_imag = probe[1].astype(jnp.float32)
    object_real = objects[:, 0].astype(jnp.float32)
    object_imag = objects[:, 1].astype(jnp.float32)
    wave_real = (probe_real * object_real - probe_imag * object_imag).astype(jnp.bfloat16)
    wave_imag = (probe_real * object_imag + probe_imag * object_real).astype(jnp.bfloat16)
    first_real = (left_product(real_table, wave_real) - left_product(imag_table, wave_imag)).astype(
        jnp.bfloat16
    )
    first_imag = (left_product(real_table, wave_imag) + left_product(imag_table, wave_real)).astype(
        jnp.bfloat16
    )
    far_real = right_product(first_real, real_table) - right_product(first_imag, imag_table)
    far_imag = right_product(first_real, imag_table) + right_product(first_imag, real_table)
    magnitude = jnp.sqrt(far_real * far_real + far_imag * far_imag)
    factor = frame_stack.astype(jnp.float32) / jnp.maximum(magnitude, 0.5)
    fixed_real = (factor * far_real).astype(jnp.bfloat16)
    fixed_imag = (factor * far_imag).astype(jnp.bfloat16)
    back_real = (
        left_product(real_table, fixed_real) + left_product(imag_table, fixed_imag)
    ).astype(jnp.bfloat16)
    back_imag = (
        left_product(real_table, fixed_imag) - left_product(imag_table, fixed_real)
    ).astype(jnp.bfloat16)
    near_real = right_product(back_real, real_table) + right_product(back_imag, imag_table)
    near_imag = right_product(back_imag, real_table) - right_product(back_real, imag_table)
    diff_real = near_real - wave_real.astype(jnp.float32)
    diff_imag = near_imag - wave_imag.astype(jnp.float32)
    step_real = probe_real * diff_real + probe_imag * diff_imag
    step_imag = probe_real * diff_imag - probe_imag * diff_real
    new_real = (object_real + step_real / scale_den).astype(jnp.bfloat16)
    new_imag = (object_imag + step_imag / scale_den).astype(jnp.bfloat16)
    return jnp.stack([new_real, new_imag], axis=1)


def local(patches, owner, column, angle_slot, probe, frames, projection):
    band_count = lax.axis_size("row")
    held_count = patches.shape[0]
    patch_size = patches.shape[-1]
    capacity = frames.shape[0] // band_count
    onehot = (owner[:, None] == jnp.arange(band_count, dtype=jnp.int32)[None, :]).astype(jnp.int32)
    order_rank = jnp.sum((jnp.cumsum(onehot, axis=0) - onehot) * onehot, axis=1)
    target = owner * capacity + order_rank
    real_table, imag_table = dft_tables(patch_size)
    probe_wide = probe.astype(jnp.float32)
    scale_den = jnp.max(probe_wide[0] * probe_wide[0] + probe_wide[1] * probe_wide[1]) + 1e-05
    fetched = lax.all_to_all(
        frames.reshape(band_count, capacity, patch_size, patch_size),
        "row",
        split_axis=0,
        concat_axis=0,
        tiled=True,
    )
    own_frames = jnp.take(
        fetched.reshape(band_count * capacity, patch_size, patch_size), target, axis=0
    )
    refined_patches = refine_batch(patches, own_frames, probe, real_table, imag_table, scale_den)

    def place(position, accumulated):
        angle_id = angle_slot[position]
        col_start = column[position]
        row_start = jnp.zeros((), jnp.int32)
        tile_delta = refined_patches[position, 0].astype(jnp.float32) - patches[position, 0].astype(
            jnp.float32
        )
        current = lax.dynamic_slice(
            accumulated, (angle_id, row_start, col_start), (1, patch_size, patch_size)
        )
        return lax.dynamic_update_slice(
            accumulated, current + tile_delta[None], (angle_id, row_start, col_start)
        )

    accumulated = lax.fori_loop(0, held_count, place, projection.astype(jnp.float32))
    regrouped = lax.all_to_all(
        accumulated.astype(jnp.bfloat16), "ang", split_axis=1, concat_axis=0, tiled=True
    )
    return (refined_patches, regrouped[:, None])


def solution(mesh):
    return jax.shard_map(
        local,
        mesh=mesh,
        in_specs=(
            P(("ang", "row"), None, None, None),
            P(("ang", "row")),
            P(("ang", "row")),
            P(("ang", "row")),
            P(),
            P(("ang", "row"), None, None),
            P("ang", "row", None),
        ),
        out_specs=(P(("ang", "row"), None, None, None), P(None, "row", "ang", None)),
        check_vma=False,
    )
```

profile of v0, /device:TPU:0, one launch (start us, length us, event | category | flops | bytes accessed | tf_op | source)
XLA Modules:
  0.0 219.2 jit_solution(16613037119159324764)
XLA Ops:
  0.7 7.4 %all-to-all-start = ((bf16[8,2,256,256]{3,2,1,0:T(8,128)(2,1)}), bf16[8,2,256,256]{3,2,1,0:T(8,128)(2,1)}, u32[]{:S(2)}, u32[]{:S(2)}) async-start(bf16[8,2,256,256]{3,2,1,0:T(8,128)(2,1)} %bitcast.101), calls=%async_computation | async-start | bytes 4194304 | tf_op jit(solution)/shard_map/all_to_all | solution.py:75
  9.0 2.5 %convert_element_type.202 = f32[2,256,2048]{2,1,0:T(8,128)} convert(bf16[2,256,2048]{2,1,0:T(8,128)(2,1)S(1)} %copy-done.3) | non-fusion elementwise | flops 1048576 | bytes 6291456 | tf_op jit(solution)/shard_map/convert_element_type | solution.py:101
  12.2 2.9 %fusion.3 = (bf16[12,256,256]{2,1,0:T(8,128)(2,1)S(1)}, bf16[12,256,256]{2,1,0:T(8,128)(2,1)S(1)}) fusion(f32[256,256]{1,0:T(8,128)S(1)} %get-tuple-element.157, f32[256,256]{1,0:T(8,128)S(1)} %get-tuple-element.156, bf16[12,2,256,256]{3,2,1,0:T(8,128)(2,1)} %param.9), kind=kLoop, calls=%fused_computation.12 | loop fusion | flops 7864320 | bytes 6815744 | tf_op jit(solution)/shard_map/convert_element_type | solution.py:34
  21.3 3.2 %fusion.14 = f32[12,256,256]{2,1,0:T(8,128)} fusion(bf16[12,256,256]{2,1,0:T(8,128)(2,1)S(1)} %subtract_convert_fusion.1), kind=kOutput, calls=%fused_computation.35 | convolution fusion | flops 403767296 | bytes 4718592 | tf_op jit(solution)/shard_map/nij,jk->nik/dot_general | solution.py:25
  27.3 3.4 %convolution_subtract_fusion = f32[12,256,256]{2,1,0:T(8,128)} fusion(f32[12,256,256]{2,1,0:T(8,128)S(1)} %fusion.16, bf16[12,256,256]{2,1,0:T(8,128)(2,1)S(1)} %add_convert_fusion.1), kind=kOutput, calls=%fused_computation.26 | convolution fusion | flops 404553728 | bytes 7864320 | tf_op jit(solution)/shard_map/nij,jk->nik/dot_general | solution.py:25
  30.7 25.7 %all-to-all-done = bf16[8,2,256,256]{3,2,1,0:T(8,128)(2,1)} async-done(((bf16[8,2,256,256]{3,2,1,0:T(8,128)(2,1)}), bf16[8,2,256,256]{3,2,1,0:T(8,128)(2,1)}, u32[]{:S(2)}, u32[]{:S(2)}) %all-to-all-start) | async-done | bytes 2097184 | tf_op jit(solution)/shard_map/all_to_all | solution.py:75
  56.4 3.4 %gather_fusion = bf16[12,256,256]{2,1,0:T(8,128)(2,1)} fusion(bf16[16,256,256]{2,1,0:T(8,128)(2,1)} %bitcast.6, s32[1024]{0:T(1024)S(1)} %pad_clamp_fusion), kind=kCustom, calls=%fused_computation | custom fusion | bytes 3145776 | tf_op jit(solution)/shard_map/jit(_take)/gather | solution.py:82
  59.9 6.5 %multiply_convert_fusion = (bf16[12,256,256]{2,1,0:T(8,128)(2,1)S(1)}, bf16[12,256,256]{2,1,0:T(8,128)(2,1)S(1)}) fusion(f32[12,256,256]{2,1,0:T(8,128)} %convolution_subtract_fusion, bf16[12,256,256]{2,1,0:T(8,128)(2,1)} %gather_fusion, pred[12]{0:T(512)(128)(4,1)S(1)} %get-tuple-element.148, f32[12,256,256]{2,1,0:T(8,128)} %fusion.14, ...), kind=kOutput, calls=%fused_computation.20 | convolution fusion | flops 413138944 | bytes 12582924 | tf_op jit(solution)/shard_map/nij,jk->nik/dot_general | solution.py:25
  77.6 3.4 %fusion.19 = (bf16[12,1,256,256]{3,2,0,1:T(8,128)(2,1)S(1)}, bf16[12,1,256,256]{3,2,0,1:T(8,128)(2,1)S(1)}) fusion(f32[]{:T(128)S(6)} %add.137, f32[12,256,256]{2,1,0:T(8,128)S(1)} %convert_subtract_fusion, f32[256,256]{1,0:T(8,128)S(1)} %copy-done.6, f32[256,256]{1,0:T(8,128)S(1)} %get-tuple-element.156, bf16[12,2,256,256]{3,2,1,0:T(8,128)(2,1)S(1)} %copy-done.2, ...), kind=kOutput, calls=%fused_computation.41 | convolution fusion | flops 417136640 | bytes 16252932 | tf_op jit(solution)/shard_map/nij,jk->nik/dot_general | solution.py:25
  81.9 100.3 %while.13 = (s32[]{:T(128)}, f32[2,256,2048]{2,1,0:T(8,128)}, s32[12]{0:T(128)S(1)}, s32[12]{0:T(128)S(1)}, bf16[12,2,256,256]{3,2,1,0:T(8,128)(2,1)S(1)}, /*ind...) while((s32[]{:T(128)}, f32[2,256,2048]{2,1,0:T(8,128)}, ...), condition=%wide.region_4.5_spmd, body=%wide.region_3.4_spmd.sunk | while | flops 262152 | bytes 1310937 | solution.py:101
  88.1 2.1 dynamic_update_slice.8
  96.5 2.1 dynamic_update_slice.8
  104.9 2.1 dynamic_update_slice.8
  113.2 2.1 dynamic_update_slice.8
  121.6 2.1 dynamic_update_slice.8
  129.9 2.1 dynamic_update_slice.8
  138.3 2.1 dynamic_update_slice.8
  146.7 2.1 dynamic_update_slice.8
  155.0 2.1 dynamic_update_slice.8
  163.4 2.1 dynamic_update_slice.8
  180.1 2.1 dynamic_update_slice.8
  182.2 6.6 %copy.93 = bf16[2,256,2048]{2,0,1:T(2,128)(2,1)S(1)} copy(f32[2,256,2048]{2,1,0:T(8,128)} %get-tuple-element.111) | data formatting | bytes 6291456 | tf_op jit(solution)/shard_map/while | solution.py:101
  188.8 28.2 %all_to_all.20 = bf16[2,256,2048]{2,0,1:T(2,128)(2,1)S(1)} all-to-all(bf16[2,256,2048]{2,0,1:T(2,128)(2,1)S(1)} %copy.93), channel_id=1, replica_groups=mesh['ang'=4,'row'=8] {'ang'}, dimensions={1} | all-to-all | bytes 4194304 | tf_op jit(solution)/shard_map/all_to_all | solution.py:102
  217.0 2.2 %copy.72 = bf16[4,2,64,2048]{3,2,1,0:T(8,128)(2,1)} copy(bf16[4,2,64,2048]{3,1,2,0:T(2,128)(2,1)S(1)} %bitcast.100) | data formatting | bytes 4194304 | tf_op jit(solution)/shard_map/all_to_all | solution.py:102
  (79 shorter events, 52.2 us)
Async XLA Ops:
  0.6 7.5 %copy-start.4 = (bf16[2,256,256]{2,1,0:T(8,128)(2,1)S(1)}, bf16[2,256,256]{2,1,0:T(8,128)(2,1)}, u32[]{:S(2)}) copy-start(bf16[2,256,256]{2,1,0:T(8,128)(2,1)} %param.13) | copy-start | bytes 786436
  0.6 7.5 %copy-start.7 = (s32[12]{0:T(128)S(1)}, s32[12]{0:T(128)}, u32[]{:S(2)}) copy-start(s32[12]{0:T(128)} %param.10) | copy-start | bytes 148
  0.7 8.3 %copy-start.3 = (bf16[2,256,2048]{2,1,0:T(8,128)(2,1)S(1)}, bf16[2,256,2048]{2,1,0:T(8,128)(2,1)}, u32[]{:S(2)}) copy-start(bf16[2,256,2048]{2,1,0:T(8,128)(2,1)} %param.15) | copy-start | bytes 6291460
  0.7 55.8 %all-to-all-start = ((bf16[8,2,256,256]{3,2,1,0:T(8,128)(2,1)}), bf16[8,2,256,256]{3,2,1,0:T(8,128)(2,1)}, u32[]{:S(2)}, u32[]{:S(2)}) async-start(bf16[8,2,256,256]{3,2,1,0:T(8,128)(2,1)} %bitcast.101), calls=%async_computation | async-start | bytes 4194304 | tf_op jit(solution)/shard_map/all_to_all | solution.py:75
  12.2 2.9 %copy-start.5 = (f32[256,256]{1,0:T(8,128)}, f32[256,256]{1,0:T(8,128)S(1)}, u32[]{:S(2)}) copy-start(f32[256,256]{1,0:T(8,128)S(1)} %get-tuple-element.157) | copy-start | bytes 786436
  26.1 1.2 copy-start
  75.7 1.9 copy-start.2
  75.7 1.9 copy-start.6
  81.2 0.7 copy-start.8
  81.2 0.7 copy-start.9
  182.2 6.6 %copy-start.1 = (bf16[12,2,256,256]{3,2,1,0:T(8,128)(2,1)}, bf16[12,2,256,256]{3,2,1,0:T(8,128)(2,1)S(1)}, u32[]{:S(2)}) copy-start(bf16[12,2,256,256]{3,2,1,0:T(8,128)(2,1)S(1)} %get-tuple-element.225) | copy-start | bytes 9437188
where the time goes:
time: 221 us; the launch traced here: 219 us
  local copies, waits for them, and re-layouts  53.8 us (24%)
  loops' own time  46.7 us (21%)
  matrix products  35.1 us (16%)
  blocking collectives  28.2 us (13%)
  waiting for transfers between devices  25.7 us (12%)
  other arithmetic  20.7 us (9%)
  starting transfers between devices  7.42 us (3%)
    another operation x1, loops' own time, local(): lax.fori_loop(0, held_count, place, projection.astype(jnp.float32))  46.7 us
    all_to_all x1, blocking collectives, local(): lax.all_to_all(accumulated.astype(jnp.bfloat16), 'ang', split_axis=1, con...  28.2 us
    all_to_all x1, waiting for transfers between devices, local(): lax.all_to_all(frames.reshape(band_count, capacity, patch_size, patch_siz...  25.7 us
    dynamic_update_slice x12, local copies, waits for them, and re-layouts, place(): lax.dynamic_update_slice(accumulated, current + tile_delta[None], (angle_...  25.4 us
    dot_general x8, matrix products, right_product(): jnp.einsum('nij,jk->nik', stacked, table, preferred_element_type=jnp.floa...  22.7 us
    add x12, other arithmetic, place(): current + tile_delta[None]  14.1 us
    dot_general x8, matrix products, left_product(): jnp.einsum('ij,njk->nik', table, stacked, preferred_element_type=jnp.floa...  12.4 us
    all_to_all x1, starting transfers between devices, local(): lax.all_to_all(frames.reshape(band_count, capacity, patch_size, patch_siz...  7.42 us
  transfers between devices with their start and end apart: 1, of which 1 were waited for; matrix products, arithmetic and copies ran while one was open for 9% of the time, Pallas kernels for 0%

commit v1 on v0

v1 whole, which is shorter than its diff:
```python
import functools
import math

import jax
import jax.numpy as jnp
import ml_dtypes
import numpy as np
from jax import lax
from jax.experimental import pallas as pl
from jax.experimental.pallas import tpu as pltpu
from jax.sharding import PartitionSpec as P

MESH = pl.DeviceIdType.MESH
LANES = 128


def tables(size):
    position = np.arange(size)
    product = position[:, None] * position[None, :] % size
    phase = product.astype(np.float32) * np.float32(2.0 * math.pi / size)
    factor = np.float32(1.0 / math.sqrt(size))
    real = (np.cos(phase) * factor).astype(ml_dtypes.bfloat16)
    imag = (-np.sin(phase) * factor).astype(ml_dtypes.bfloat16)
    return np.block([[real, -imag], [imag, real]]), np.block([[real, imag], [-imag, real]])


def partner(me, step, count):
    result = 0
    bit = 1
    while bit < count:
        result = result + bit * lax.rem(lax.div(me, bit) + lax.div(step, bit), 2)
        bit *= 2
    return result


def i32(value):
    return jnp.int32(value)


def refine_kernel(
    n_a, n_r, capacity,
    owner_ref, column_ref, angle_ref, probe_ref, fwd_ref, inv_ref, patches, frames, projection,
    slots_out, delta_out, projection_out, info_out,
    held, frame_in, stage, delta, info,
    held_sem, own_sem, frame_send, frame_recv, stage_sem,
    delta_send, delta_recv, proj_send, proj_recv, info_send, info_recv,
):
    a, r = lax.axis_index("ang"), lax.axis_index("row")
    count, size = patches.shape[0], patches.shape[-1]
    slots = n_r * capacity
    rows = size // n_a

    barrier = pltpu.get_barrier_semaphore()
    for k in range(1, n_r):
        pl.semaphore_signal(
            barrier, inc=1, device_id=(a, partner(r, i32(k), n_r)), device_id_type=MESH
        )
    for j in range(1, n_a):
        pl.semaphore_signal(
            barrier, inc=1, device_id=(partner(a, i32(j), n_a), r), device_id_type=MESH
        )

    load = pltpu.make_async_copy(patches, held, held_sem)
    load.start()

    def own_frame(c):
        return pltpu.make_async_copy(
            frames.at[r * capacity + c], frame_in.at[c], own_sem.at[c]
        )

    def send_frame(s):
        step, c = lax.div(s, capacity), lax.rem(s, capacity)
        other = partner(r, step, n_r)
        return pltpu.make_async_remote_copy(
            src_ref=frames.at[other * capacity + c],
            dst_ref=frame_in.at[s],
            send_sem=frame_send.at[s],
            recv_sem=frame_recv.at[s],
            device_id=(a, other),
            device_id_type=MESH,
        )

    def send_projection(j):
        other = partner(a, i32(j), n_a)
        return pltpu.make_async_remote_copy(
            src_ref=projection.at[:, pl.ds(other * rows, rows), :],
            dst_ref=projection_out.at[j],
            send_sem=proj_send.at[j],
            recv_sem=proj_recv.at[j],
            device_id=(other, r),
            device_id_type=MESH,
        )

    def send_info(j):
        return pltpu.make_async_remote_copy(
            src_ref=info,
            dst_ref=info_out.at[j],
            send_sem=info_send.at[j],
            recv_sem=info_recv.at[j],
            device_id=(partner(a, i32(j), n_a), r),
            device_id_type=MESH,
        )

    def send_delta(j, s):
        other = partner(a, i32(j), n_a)
        return pltpu.make_async_remote_copy(
            src_ref=delta.at[s, pl.ds(other * rows, rows), :],
            dst_ref=delta_out.at[j, s],
            send_sem=delta_send.at[j, s],
            recv_sem=delta_recv.at[j, s],
            device_id=(other, r),
            device_id_type=MESH,
        )

    def own_delta(s):
        return pltpu.make_async_copy(
            delta.at[s, pl.ds(a * rows, rows), :], delta_out.at[0, s], delta_recv.at[0, s]
        )

    own_projection = pltpu.make_async_copy(
        projection.at[:, pl.ds(a * rows, rows), :], projection_out.at[0], proj_recv.at[0]
    )
    own_info = pltpu.make_async_copy(info, info_out.at[0], info_recv.at[0])

    for c in range(capacity):
        own_frame(c).start()

    owners = [owner_ref[p] for p in range(count)]
    row_id = lax.broadcasted_iota(jnp.int32, info.shape, 0)
    lane_id = lax.broadcasted_iota(jnp.int32, info.shape, 1)
    packed = jnp.zeros(info.shape, jnp.int32)
    for p in range(count):
        rank = i32(0)
        for q in range(p):
            rank = rank + jnp.where(owners[q] == owners[p], 1, 0)
        slot = partner(r, owners[p], n_r) * capacity + rank
        here = lane_id == p
        packed = jnp.where(here & (row_id == 0), slot, packed)
        packed = jnp.where(here & (row_id == 1), column_ref[p], packed)
        packed = jnp.where(here & (row_id == 2), angle_ref[p], packed)
    info[...] = packed

    pl.semaphore_wait(barrier, n_r - 1 + n_a - 1)

    def start_frames(i, carry):
        send_frame(slots - 1 - i).start()
        return carry

    lax.fori_loop(0, slots - capacity, start_frames, 0)
    for j in range(1, n_a):
        send_projection(j).start()
        send_info(j).start()
    own_projection.start()
    own_info.start()

    probe_real = probe_ref[0].astype(jnp.float32)
    probe_imag = probe_ref[1].astype(jnp.float32)
    peak = jnp.max(probe_real * probe_real + probe_imag * probe_imag)
    scale = 1.0 / (jnp.full((1, size), peak, jnp.float32) + 1e-05)

    load.wait()
    for c in range(capacity):
        own_frame(c).wait()

    def dot(left, right):
        return jnp.dot(left, right, preferred_element_type=jnp.float32)

    def one_slot(s, carry):
        owner = partner(r, lax.div(s, capacity), n_r)
        wanted = lax.rem(s, capacity)
        seen, position = i32(0), i32(0)
        for p in range(count):
            hit = owner_ref[p] == owner
            position = jnp.where(hit & (seen == wanted), i32(p), position)
            seen = seen + jnp.where(hit, 1, 0)

        pr = probe_ref[0].astype(jnp.float32)
        pi = probe_ref[1].astype(jnp.float32)
        patch_real = held[position, 0].astype(jnp.float32)
        patch_imag = held[position, 1].astype(jnp.float32)
        wave_real = (pr * patch_real - pi * patch_imag).astype(jnp.bfloat16)
        wave_imag = (pr * patch_imag + pi * patch_real).astype(jnp.bfloat16)
        first = dot(fwd_ref[...], jnp.concatenate([wave_real, wave_imag], axis=0))
        first = first.astype(jnp.bfloat16)
        far = dot(jnp.concatenate([first[:size], first[size:]], axis=1), inv_ref[...])
        far_real, far_imag = far[:, :size], far[:, size:]

        @pl.when(s >= capacity)
        def _():
            send_frame(s).wait_recv()

        power = jnp.maximum(far_real * far_real + far_imag * far_imag, 0.25)
        factor = frame_in[s].astype(jnp.float32) * lax.rsqrt(power)
        fixed_real = (factor * far_real).astype(jnp.bfloat16)
        fixed_imag = (factor * far_imag).astype(jnp.bfloat16)
        back = dot(inv_ref[...], jnp.concatenate([fixed_real, fixed_imag], axis=0))
        back = back.astype(jnp.bfloat16)
        near = dot(jnp.concatenate([back[:size], back[size:]], axis=1), fwd_ref[...])
        diff_real = near[:, :size] - wave_real.astype(jnp.float32)
        diff_imag = near[:, size:] - wave_imag.astype(jnp.float32)
        new_real = (patch_real + (pr * diff_real + pi * diff_imag) * scale).astype(jnp.bfloat16)
        new_imag = (patch_imag + (pr * diff_imag - pi * diff_real) * scale).astype(jnp.bfloat16)
        stage[s, 0] = new_real
        stage[s, 1] = new_imag
        delta[s] = (new_real.astype(jnp.float32) - patch_real).astype(jnp.bfloat16)
        for j in range(1, n_a):
            send_delta(j, s).start()
        own_delta(s).start()
        pltpu.make_async_copy(stage.at[s], slots_out.at[s], stage_sem.at[s]).start()
        return carry

    lax.fori_loop(0, slots, one_slot, 0)

    def finish(s, carry):
        @pl.when(s >= capacity)
        def _():
            send_frame(s).wait_send()

        for j in range(1, n_a):
            send_delta(j, s).wait_send()
            send_delta(j, s).wait_recv()
        own_delta(s).wait()
        pltpu.make_async_copy(stage.at[s], slots_out.at[s], stage_sem.at[s]).wait()
        return carry

    lax.fori_loop(0, slots, finish, 0)
    for j in range(1, n_a):
        send_projection(j).wait()
        send_info(j).wait()
    own_projection.wait()
    own_info.wait()


def place_kernel(
    angles, info_ref, projection_ref, delta_ref, slots_ref, sinogram_ref, refined_ref,
    total, sems,
):
    step = pl.program_id(0)
    last = pl.num_programs(0) - 1
    count = refined_ref.shape[0]
    rows, width = projection_ref.shape[2], projection_ref.shape[3]
    size = delta_ref.shape[-1]
    span = size + LANES

    def move(p):
        return pltpu.make_async_copy(
            slots_ref.at[info_ref[0, 0, p]], refined_ref.at[p], sems.at[p]
        )

    @pl.when(step == 0)
    def _():
        for p in range(count):
            move(p).start()

    for angle in range(angles):
        total[angle, :, :width] = projection_ref[0, angle].astype(jnp.float32)

    def place(p, carry):
        slot, column, angle = info_ref[step, 0, p], info_ref[step, 1, p], info_ref[step, 2, p]
        tile = lax.div(column, LANES)
        piece = delta_ref[0, slot].astype(jnp.float32)
        piece = jnp.concatenate([piece, jnp.zeros((rows, LANES), jnp.float32)], axis=1)
        piece = pltpu.roll(piece, lax.rem(column, LANES), 1)
        where = pl.ds(pl.multiple_of(tile * LANES, LANES), span)
        total[angle, :, where] += piece
        return carry

    lax.fori_loop(0, count, place, 0)
    for angle in range(angles):
        sinogram_ref[angle, 0] = total[angle, :, :width].astype(sinogram_ref.dtype)

    @pl.when(step == last)
    def _():
        for p in range(count):
            move(p).wait()


def local(n_a, n_r, patches, owner, column, angle_slot, probe, frames, projection):
    count, _, size, _ = patches.shape
    capacity = frames.shape[0] // n_r
    angles, _, width = projection.shape
    slots = n_r * capacity
    rows = size // n_a
    fwd, inv = tables(size)
    bf16 = jnp.bfloat16
    vmem = pl.BlockSpec(memory_space=pltpu.VMEM)
    smem = pl.BlockSpec(memory_space=pltpu.SMEM)
    hbm = pl.BlockSpec(memory_space=pl.ANY)
    dma = pltpu.SemaphoreType.DMA
    in_slots, deltas, projections, info = pl.pallas_call(
        functools.partial(refine_kernel, n_a, n_r, capacity),
        out_shape=(
            jax.ShapeDtypeStruct((slots, 2, size, size), bf16),
            jax.ShapeDtypeStruct((n_a, slots, rows, size), bf16),
            jax.ShapeDtypeStruct((n_a, angles, rows, width), bf16),
            jax.ShapeDtypeStruct((n_a, 8, LANES), jnp.int32),
        ),
        in_specs=[smem] * 3 + [vmem] * 3 + [hbm] * 3,
        out_specs=(hbm,) * 4,
        scratch_shapes=[
            pltpu.VMEM((count, 2, size, size), bf16),
            pltpu.VMEM((slots, size, size), bf16),
            pltpu.VMEM((slots, 2, size, size), bf16),
            pltpu.VMEM((slots, size, size), bf16),
            pltpu.VMEM((8, LANES), jnp.int32),
            dma,
            dma((capacity,)),
            dma((slots,)),
            dma((slots,)),
            dma((slots,)),
            dma((n_a, slots)),
            dma((n_a, slots)),
            dma((n_a,)),
            dma((n_a,)),
            dma((n_a,)),
            dma((n_a,)),
        ],
        compiler_params=pltpu.CompilerParams(
            collective_id=0, has_side_effects=True, vmem_limit_bytes=56 * 2**20
        ),
        name="refine",
    )(owner, column, angle_slot, probe, jnp.asarray(fwd), jnp.asarray(inv), patches, frames, projection)

    a = lax.axis_index("ang")
    mine = jnp.reshape(a, (1,)).astype(jnp.int32)

    def source(me, i):
        return partner(me, i, n_a)

    sinogram, refined = pl.pallas_call(
        functools.partial(placed, angles),
        grid_spec=pltpu.PrefetchScalarGridSpec(
            num_scalar_prefetch=1,
            grid=(n_a,),
            in_specs=[
                smem,
                pl.BlockSpec((1, angles, rows, width), lambda i, me: (i, 0, 0, 0)),
                pl.BlockSpec((1, slots, rows, size), lambda i, me: (i, 0, 0, 0)),
                hbm,
            ],
            out_specs=(
                pl.BlockSpec(
                    (angles, 1, rows, width), lambda i, me: (source(me[0], i), 0, 0, 0)
                ),
                hbm,
            ),
            scratch_shapes=[
                pltpu.VMEM((angles, rows, width + LANES), jnp.float32),
                dma((count,)),
            ],
        ),
        out_shape=(
            jax.ShapeDtypeStruct((n_a * angles, 1, rows, width), bf16),
            jax.ShapeDtypeStruct((count, 2, size, size), bf16),
        ),
        compiler_params=pltpu.CompilerParams(vmem_limit_bytes=32 * 2**20),
        name="place",
    )(mine, info, projections, deltas, in_slots)
    return refined, sinogram


def placed(angles, me_ref, *refs):
    place_kernel(angles, *refs)


def solution(mesh):
    return jax.shard_map(
        functools.partial(local, mesh.shape["ang"], mesh.shape["row"]),
        mesh=mesh,
        in_specs=(
            P(("ang", "row"), None, None, None),
            P(("ang", "row")),
            P(("ang", "row")),
            P(("ang", "row")),
            P(),
            P(("ang", "row"), None, None),
            P("ang", "row", None),
        ),
        out_specs=(P(("ang", "row"), None, None, None), P(None, "row", "ang", None)),
        check_vma=False,
    )
```

time: 221 us -> 87.9 us (0.40)
  Pallas kernels: 0 us -> 80.8 us
  local copies, waits for them, and re-layouts: 53.8 us -> 6.08 us
  loops' own time: 46.7 us -> 0 us
  matrix products: 35.1 us -> 0 us
  blocking collectives: 28.2 us -> 0 us
  waiting for transfers between devices: 25.7 us -> 0 us
  other arithmetic: 20.7 us -> 0 us
  starting transfers between devices: 7.42 us -> 0 us
    pallas_call x0 -> x2, Pallas kernels: none -> 80.8 us  [the longest x1 73.4 us: local(): pl.pallas_call(functools.partial(refine_kernel, n_a, n_r, capacity), out_...]
    another operation x1 -> x0, loops' own time: 46.7 us -> none  [local(): lax.fori_loop(0, held_count, place, projection.astype(jnp.float32))]
    dot_general x16 -> x0, matrix products: 35.1 us -> none  [the longest x8 22.7 us: right_product(): jnp.einsum('nij,jk->nik', stacked, table, preferred_element_type=jnp.floa...]
    all_to_all x1 -> x0, blocking collectives: 28.2 us -> none  [local(): lax.all_to_all(accumulated.astype(jnp.bfloat16), 'ang', split_axis=1, con...]
    all_to_all x1 -> x0, waiting for transfers between devices: 25.7 us -> none  [local(): lax.all_to_all(frames.reshape(band_count, capacity, patch_size, patch_siz...]
    dynamic_update_slice x12 -> x0, local copies, waits for them, and re-layouts: 25.4 us -> none  [place(): lax.dynamic_update_slice(accumulated, current + tile_delta[None], (angle_...]
    add x12 -> x0, other arithmetic: 14.1 us -> none  [place(): current + tile_delta[None]]
    dynamic_slice x24 -> x0, local copies, waits for them, and re-layouts: 14 us -> none  [the longest x12 7.06 us: place(): col_start = column[position]]
  transfers between devices with their start and end apart: 1 -> 0, of which waited for: 1 -> 0; matrix products, arithmetic and copies ran while one was open for 9% -> 0% of each run, Pallas kernels for 0% -> 0%
where the time goes in v1:
time: 87.9 us; the launch traced here: 87.6 us
  Pallas kernels  80.8 us (92%)
  local copies, waits for them, and re-layouts  6.08 us (7%)
    pallas_call x1, Pallas kernels, local(): pl.pallas_call(functools.partial(refine_kernel, n_a, n_r, capacity), out_...  73.4 us
    pallas_call x1, Pallas kernels, local(): pl.pallas_call(functools.partial(placed, angles), grid_spec=pltpu.Prefetc...  7.47 us
    unnamed x8, local copies, waits for them, and re-layouts  6.08 us

profile of v1, /device:TPU:0, one launch (start us, length us, event | category | flops | bytes accessed | tf_op | source)
XLA Modules:
  0.0 87.6 jit_solution(17936219896749360759)
XLA Ops:
  0.6 73.4 %refine.1 = (bf16[16,2,256,256]{3,2,1,0:T(8,128)(2,1)}, bf16[4,16,64,256]{3,2,1,0:T(8,128)(2,1)}, bf16[4,2,64,2048]{3,2,1,0:T(8,128)(2,1)}, s32[4,8,128]{2,1,0:T(8,128)}) custom-call(s32[12]{0:T(128)} %owner_ref.1, s32[12]{0:T(128)} %column_ref.1, s32[12]{0:T(128)} %angle_ref.1, bf16[2,256,256]{2,1,0:T(8,128)(2,1)} %probe_ref.1, ...), custom_call_target="tpu_custom_call" | custom-call | tf_op jit(solution)/shard_map/refine/pallas_call | solution.py:290
  74.0 0.0 copy-start
  74.0 2.2 %copy-done = bf16[16,2,256,256]{3,2,1,0:T(8,128)(2,1)S(1)} copy-done((bf16[16,2,256,256]{3,2,1,0:T(8,128)(2,1)S(1)}, bf16[16,2,256,256]{3,2,1,0:T(8,128)(2,1)}, u32[]{:S(2)}) %copy-start) | copy-done | bytes 4194328
  76.2 0.0 copy-start.1
  76.2 1.6 %copy-done.1 = bf16[4,16,64,256]{3,2,1,0:T(8,128)(2,1)S(1)} copy-done((bf16[4,16,64,256]{3,2,1,0:T(8,128)(2,1)S(1)}, bf16[4,16,64,256]{3,2,1,0:T(8,128)(2,1)}, u32[]{:S(2)}) %copy-start.1) | copy-done | bytes 2097176
  77.8 0.0 copy-start.2
  77.8 1.6 %copy-done.2 = bf16[4,2,64,2048]{3,2,1,0:T(8,128)(2,1)S(1)} copy-done((bf16[4,2,64,2048]{3,2,1,0:T(8,128)(2,1)S(1)}, bf16[4,2,64,2048]{3,2,1,0:T(8,128)(2,1)}, u32[]{:S(2)}) %copy-start.2) | copy-done | bytes 2097176
  79.4 0.0 copy-start.3
  79.4 0.7 copy-done.3
  80.1 7.5 %place.1 = (bf16[8,1,64,2048]{3,2,1,0:T(8,128)(2,1)}, bf16[12,2,256,256]{3,2,1,0:T(8,128)(2,1)}) custom-call(s32[1]{0:T(128)} %bitcast.me_ref, s32[4,8,128]{2,1,0:T(8,128)S(1)} %copy-done.3, bf16[4,2,64,2048]{3,2,1,0:T(8,128)(2,1)S(1)} %copy-done.2, bf16[4,16,64,256]{3,2,1,0:T(8,128)(2,1)S(1)} %copy-done.1, bf16[16,2,256,256]{3,2,1,0:T(8,128)(2,1)S(1)} %copy-done), custom_call_target="tpu_custom_call" | custom-call | tf_op jit(solution)/shard_map/place/pallas_call | solution.py:330
Async XLA Ops:
  74.0 2.2 %copy-start = (bf16[16,2,256,256]{3,2,1,0:T(8,128)(2,1)S(1)}, bf16[16,2,256,256]{3,2,1,0:T(8,128)(2,1)}, u32[]{:S(2)}) copy-start(bf16[16,2,256,256]{3,2,1,0:T(8,128)(2,1)} %get-tuple-element.11.refs_3_) | copy-start | bytes 12582916
  76.2 1.6 %copy-start.1 = (bf16[4,16,64,256]{3,2,1,0:T(8,128)(2,1)S(1)}, bf16[4,16,64,256]{3,2,1,0:T(8,128)(2,1)}, u32[]{:S(2)}) copy-start(bf16[4,16,64,256]{3,2,1,0:T(8,128)(2,1)} %get-tuple-element.10.refs_2_) | copy-start | bytes 6291460
  77.8 1.6 %copy-start.2 = (bf16[4,2,64,2048]{3,2,1,0:T(8,128)(2,1)S(1)}, bf16[4,2,64,2048]{3,2,1,0:T(8,128)(2,1)}, u32[]{:S(2)}) copy-start(bf16[4,2,64,2048]{3,2,1,0:T(8,128)(2,1)} %get-tuple-element.9.refs_1_) | copy-start | bytes 6291460
  79.4 0.7 copy-start.3

commit v2 on v1

--- a/solution.py
+++ b/solution.py
@@ -12,6 +12,7 @@
 
 MESH = pl.DeviceIdType.MESH
 LANES = 128
+WINDOW = 6
 
 
 def tables(size):
@@ -31,6 +32,15 @@
         result = result + bit * lax.rem(lax.div(me, bit) + lax.div(step, bit), 2)
         bit *= 2
     return result
+
+
+def step_of(slot, capacity, count):
+    turn = lax.div(slot, capacity)
+    return lax.div(turn, 2) + lax.rem(turn, 2) * (count // 2)
+
+
+def turn_of(step, count):
+    return lax.rem(step, count // 2) * 2 + lax.div(step, count // 2)
 
 
 def i32(value):
@@ -49,6 +59,7 @@
     count, size = patches.shape[0], patches.shape[-1]
     slots = n_r * capacity
     rows = size // n_a
+    angles = projection.shape[0]
 
     barrier = pltpu.get_barrier_semaphore()
     for k in range(1, n_r):
@@ -69,8 +80,8 @@
         )
 
     def send_frame(s):
-        step, c = lax.div(s, capacity), lax.rem(s, capacity)
-        other = partner(r, step, n_r)
+        c = lax.rem(s, capacity)
+        other = partner(r, step_of(s, capacity, n_r), n_r)
         return pltpu.make_async_remote_copy(
             src_ref=frames.at[other * capacity + c],
             dst_ref=frame_in.at[s],
@@ -80,13 +91,13 @@
             device_id_type=MESH,
         )
 
-    def send_projection(j):
+    def send_projection(j, angle):
         other = partner(a, i32(j), n_a)
         return pltpu.make_async_remote_copy(
-            src_ref=projection.at[:, pl.ds(other * rows, rows), :],
-            dst_ref=projection_out.at[j],
-            send_sem=proj_send.at[j],
-            recv_sem=proj_recv.at[j],
+            src_ref=projection.at[angle, pl.ds(other * rows, rows), :],
+            dst_ref=projection_out.at[j, angle],
+            send_sem=proj_send.at[j, angle],
+            recv_sem=proj_recv.at[j, angle],
             device_id=(other, r),
             device_id_type=MESH,
         )
@@ -118,7 +129,7 @@
         )
 
     own_projection = pltpu.make_async_copy(
-        projection.at[:, pl.ds(a * rows, rows), :], projection_out.at[0], proj_recv.at[0]
+        projection.at[:, pl.ds(a * rows, rows), :], projection_out.at[0], proj_recv.at[0, 0]
     )
     own_info = pltpu.make_async_copy(info, info_out.at[0], info_recv.at[0])
 
@@ -133,7 +144,7 @@
         rank = i32(0)
         for q in range(p):
             rank = rank + jnp.where(owners[q] == owners[p], 1, 0)
-        slot = partner(r, owners[p], n_r) * capacity + rank
+        slot = turn_of(partner(r, owners[p], n_r), n_r) * capacity + rank
         here = lane_id == p
         packed = jnp.where(here & (row_id == 0), slot, packed)
         packed = jnp.where(here & (row_id == 1), column_ref[p], packed)
@@ -142,13 +153,14 @@
 
     pl.semaphore_wait(barrier, n_r - 1 + n_a - 1)
 
-    def start_frames(i, carry):
-        send_frame(slots - 1 - i).start()
-        return carry
-
-    lax.fori_loop(0, slots - capacity, start_frames, 0)
+    window = min(WINDOW, slots - capacity)
+    pieces = [(j, angle) for angle in range(angles) for j in range(n_a - 1, 0, -1)]
+    for i in range(max(window, len(pieces))):
+        if i < window:
+            send_frame(i32(capacity + i)).start()
+        if i < len(pieces):
+            send_projection(*pieces[i]).start()
     for j in range(1, n_a):
-        send_projection(j).start()
         send_info(j).start()
     own_projection.start()
     own_info.start()
@@ -166,7 +178,7 @@
         return jnp.dot(left, right, preferred_element_type=jnp.float32)
 
     def one_slot(s, carry):
-        owner = partner(r, lax.div(s, capacity), n_r)
+        owner = partner(r, step_of(s, capacity, n_r), n_r)
         wanted = lax.rem(s, capacity)
         seen, position = i32(0), i32(0)
         for p in range(count):
@@ -188,6 +200,10 @@
         @pl.when(s >= capacity)
         def _():
             send_frame(s).wait_recv()
+
+        @pl.when((s >= capacity) & (s + window < slots))
+        def _():
+            send_frame(s + window).start()
 
         power = jnp.maximum(far_real * far_real + far_imag * far_imag, 0.25)
         factor = frame_in[s].astype(jnp.float32) * lax.rsqrt(power)
@@ -225,7 +241,8 @@
 
     lax.fori_loop(0, slots, finish, 0)
     for j in range(1, n_a):
-        send_projection(j).wait()
+        for angle in range(angles):
+            send_projection(j, angle).wait()
         send_info(j).wait()
     own_projection.wait()
     own_info.wait()
@@ -233,7 +250,7 @@
 
 def place_kernel(
     angles, info_ref, projection_ref, delta_ref, slots_ref, sinogram_ref, refined_ref,
-    total, sems,
+    total, bounce, in_sem, out_sem,
 ):
     step = pl.program_id(0)
     last = pl.num_programs(0) - 1
@@ -242,15 +259,18 @@
     size = delta_ref.shape[-1]
     span = size + LANES
 
-    def move(p):
+    def fetch(p):
         return pltpu.make_async_copy(
-            slots_ref.at[info_ref[0, 0, p]], refined_ref.at[p], sems.at[p]
-        )
+            slots_ref.at[info_ref[0, 0, p]], bounce.at[p], in_sem.at[p]
+        )
+
+    def store(p):
+        return pltpu.make_async_copy(bounce.at[p], refined_ref.at[p], out_sem.at[p])
 
     @pl.when(step == 0)
     def _():
         for p in range(count):
-            move(p).start()
+            fetch(p).start()
 
     for angle in range(angles):
         total[angle, :, :width] = projection_ref[0, angle].astype(jnp.float32)
@@ -265,14 +285,20 @@
         total[angle, :, where] += piece
         return carry
 
-    lax.fori_loop(0, count, place, 0)
+    lax.fori_loop(0, count, place, 0, unroll=True)
+    @pl.when(step == 0)
+    def _():
+        for p in range(count):
+            fetch(p).wait()
+            store(p).start()
+
     for angle in range(angles):
         sinogram_ref[angle, 0] = total[angle, :, :width].astype(sinogram_ref.dtype)
 
     @pl.when(step == last)
     def _():
         for p in range(count):
-            move(p).wait()
+            store(p).wait()
 
 
 def local(n_a, n_r, patches, owner, column, angle_slot, probe, frames, projection):
@@ -310,8 +336,8 @@
             dma((slots,)),
             dma((n_a, slots)),
             dma((n_a, slots)),
-            dma((n_a,)),
-            dma((n_a,)),
+            dma((n_a, angles)),
+            dma((n_a, angles)),
             dma((n_a,)),
             dma((n_a,)),
         ],
@@ -346,6 +372,8 @@
             ),
             scratch_shapes=[
                 pltpu.VMEM((angles, rows, width + LANES), jnp.float32),
+                pltpu.VMEM((count, 2, size, size), bf16),
+                dma((count,)),
                 dma((count,)),
             ],
         ),
@@ -353,7 +381,7 @@
             jax.ShapeDtypeStruct((n_a * angles, 1, rows, width), bf16),
             jax.ShapeDtypeStruct((count, 2, size, size), bf16),
         ),
-        compiler_params=pltpu.CompilerParams(vmem_limit_bytes=32 * 2**20),
+        compiler_params=pltpu.CompilerParams(vmem_limit_bytes=60 * 2**20),
         name="place",
     )(mine, info, projections, deltas, in_slots)
     return refined, sinogram

time: 87.9 us -> 66.8 us (0.76)
  the two profiles are of different devices: /device:TPU:0 before, /device:TPU:17 now
where the time goes in v2:
time: 66.8 us; the launch traced here: 66.6 us
  Pallas kernels  66 us (99%)
    pallas_call x1, Pallas kernels, local(): pl.pallas_call(functools.partial(refine_kernel, n_a, n_r, capacity), out_...  59 us
    pallas_call x1, Pallas kernels, local(): pl.pallas_call(functools.partial(placed, angles), grid_spec=pltpu.Prefetc...  6.93 us

profile of v2, /device:TPU:17, one launch (start us, length us, event | category | flops | bytes accessed | tf_op | source)
XLA Modules:
  0.0 66.6 jit_solution(8081699672295537145)
XLA Ops:
  0.6 59.0 %refine.1 = (bf16[16,2,256,256]{3,2,1,0:T(8,128)(2,1)}, bf16[4,16,64,256]{3,2,1,0:T(8,128)(2,1)}, bf16[4,2,64,2048]{3,2,1,0:T(8,128)(2,1)}, s32[4,8,128]{2,1,0:T(8,128)}) custom-call(s32[12]{0:T(128)} %owner_ref.1, s32[12]{0:T(128)} %column_ref.1, s32[12]{0:T(128)} %angle_ref.1, bf16[2,256,256]{2,1,0:T(8,128)(2,1)} %probe_ref.1, ...), custom_call_target="tpu_custom_call" | custom-call | tf_op jit(solution)/shard_map/refine/pallas_call | solution.py:316
  59.7 6.9 %place.1 = (bf16[8,1,64,2048]{3,2,1,0:T(8,128)(2,1)}, bf16[12,2,256,256]{3,2,1,0:T(8,128)(2,1)}) custom-call(s32[1]{0:T(128)} %bitcast.me_ref, s32[4,8,128]{2,1,0:T(8,128)} %get-tuple-element.8.refs_0_, bf16[4,2,64,2048]{3,2,1,0:T(8,128)(2,1)} %get-tuple-element.9.refs_1_, bf16[4,16,64,256]{3,2,1,0:T(8,128)(2,1)} %get-tuple-element.10.refs_2_, ...), custom_call_target="tpu_custom_call" | custom-call | tf_op jit(solution)/shard_map/place/pallas_call | solution.py:356

commit v3 on v2

--- a/solution.py
+++ b/solution.py
@@ -12,7 +12,6 @@
 
 MESH = pl.DeviceIdType.MESH
 LANES = 128
-WINDOW = 6
 
 
 def tables(size):
@@ -49,9 +48,9 @@
 
 def refine_kernel(
     n_a, n_r, capacity,
-    owner_ref, column_ref, angle_ref, probe_ref, fwd_ref, inv_ref, patches, frames, projection,
+    owner_ref, column_ref, angle_ref, probe, fwd, inv, patches, frames, projection,
     slots_out, delta_out, projection_out, info_out,
-    held, frame_in, stage, delta, info,
+    held, probe_ref, fwd_ref, inv_ref, far_ref, frame_in, stage, delta, info,
     held_sem, own_sem, frame_send, frame_recv, stage_sem,
     delta_send, delta_recv, proj_send, proj_recv, info_send, info_recv,
 ):
@@ -71,8 +70,14 @@
             barrier, inc=1, device_id=(partner(a, i32(j), n_a), r), device_id_type=MESH
         )
 
-    load = pltpu.make_async_copy(patches, held, held_sem)
-    load.start()
+    loads = [
+        pltpu.make_async_copy(source, target, held_sem.at[i])
+        for i, (source, target) in enumerate(
+            [(probe, probe_ref), (fwd, fwd_ref), (inv, inv_ref), (patches, held)]
+        )
+    ]
+    for load in loads:
+        load.start()
 
     def own_frame(c):
         return pltpu.make_async_copy(
@@ -153,7 +158,7 @@
 
     pl.semaphore_wait(barrier, n_r - 1 + n_a - 1)
 
-    window = min(WINDOW, slots - capacity)
+    window = slots - capacity
     pieces = [(j, angle) for angle in range(angles) for j in range(n_a - 1, 0, -1)]
     for i in range(max(window, len(pieces))):
         if i < window:
@@ -165,17 +170,35 @@
     own_projection.start()
     own_info.start()
 
+    for load in loads:
+        load.wait()
     probe_real = probe_ref[0].astype(jnp.float32)
     probe_imag = probe_ref[1].astype(jnp.float32)
     peak = jnp.max(probe_real * probe_real + probe_imag * probe_imag)
     scale = 1.0 / (jnp.full((1, size), peak, jnp.float32) + 1e-05)
 
-    load.wait()
+    def dot(left, right):
+        return jnp.dot(left, right, preferred_element_type=jnp.float32)
+
+    def wave_of(position):
+        pr = probe_ref[0].astype(jnp.float32)
+        pi = probe_ref[1].astype(jnp.float32)
+        patch_real = held[position, 0].astype(jnp.float32)
+        patch_imag = held[position, 1].astype(jnp.float32)
+        wave_real = (pr * patch_real - pi * patch_imag).astype(jnp.bfloat16)
+        wave_imag = (pr * patch_imag + pi * patch_real).astype(jnp.bfloat16)
+        return pr, pi, patch_real, patch_imag, wave_real, wave_imag
+
+    def forward(p, carry):
+        wave_real, wave_imag = wave_of(p)[-2:]
+        first = dot(fwd_ref[...], jnp.concatenate([wave_real, wave_imag], axis=0))
+        first = first.astype(jnp.bfloat16)
+        far_ref[p] = dot(jnp.concatenate([first[:size], first[size:]], axis=1), inv_ref[...])
+        return carry
+
+    lax.fori_loop(0, count, forward, 0)
     for c in range(capacity):
         own_frame(c).wait()
-
-    def dot(left, right):
-        return jnp.dot(left, right, preferred_element_type=jnp.float32)
 
     def one_slot(s, carry):
         owner = partner(r, step_of(s, capacity, n_r), n_r)
@@ -186,24 +209,12 @@
             position = jnp.where(hit & (seen == wanted), i32(p), position)
             seen = seen + jnp.where(hit, 1, 0)
 
-        pr = probe_ref[0].astype(jnp.float32)
-        pi = probe_ref[1].astype(jnp.float32)
-        patch_real = held[position, 0].astype(jnp.float32)
-        patch_imag = held[position, 1].astype(jnp.float32)
-        wave_real = (pr * patch_real - pi * patch_imag).astype(jnp.bfloat16)
-        wave_imag = (pr * patch_imag + pi * patch_real).astype(jnp.bfloat16)
-        first = dot(fwd_ref[...], jnp.concatenate([wave_real, wave_imag], axis=0))
-        first = first.astype(jnp.bfloat16)
-        far = dot(jnp.concatenate([first[:size], first[size:]], axis=1), inv_ref[...])
-        far_real, far_imag = far[:, :size], far[:, size:]
+        pr, pi, patch_real, patch_imag, wave_real, wave_imag = wave_of(position)
+        far_real, far_imag = far_ref[position, :, :size], far_ref[position, :, size:]
 
         @pl.when(s >= capacity)
         def _():
             send_frame(s).wait_recv()
-
-        @pl.when((s >= capacity) & (s + window < slots))
-        def _():
-            send_frame(s + window).start()
 
         power = jnp.maximum(far_real * far_real + far_imag * far_imag, 0.25)
         factor = frame_in[s].astype(jnp.float32) * lax.rsqrt(power)
@@ -309,7 +320,6 @@
     rows = size // n_a
     fwd, inv = tables(size)
     bf16 = jnp.bfloat16
-    vmem = pl.BlockSpec(memory_space=pltpu.VMEM)
     smem = pl.BlockSpec(memory_space=pltpu.SMEM)
     hbm = pl.BlockSpec(memory_space=pl.ANY)
     dma = pltpu.SemaphoreType.DMA
@@ -321,15 +331,19 @@
             jax.ShapeDtypeStruct((n_a, angles, rows, width), bf16),
             jax.ShapeDtypeStruct((n_a, 8, LANES), jnp.int32),
         ),
-        in_specs=[smem] * 3 + [vmem] * 3 + [hbm] * 3,
+        in_specs=[smem] * 3 + [hbm] * 6,
         out_specs=(hbm,) * 4,
         scratch_shapes=[
             pltpu.VMEM((count, 2, size, size), bf16),
+            pltpu.VMEM((2, size, size), bf16),
+            pltpu.VMEM(fwd.shape, bf16),
+            pltpu.VMEM(inv.shape, bf16),
+            pltpu.VMEM((count, size, 2 * size), jnp.float32),
             pltpu.VMEM((slots, size, size), bf16),
             pltpu.VMEM((slots, 2, size, size), bf16),
             pltpu.VMEM((slots, size, size), bf16),
             pltpu.VMEM((8, LANES), jnp.int32),
-            dma,
+            dma((4,)),
             dma((capacity,)),
             dma((slots,)),
             dma((slots,)),

time: 66.8 us -> 64.8 us (0.970)
  the two profiles are of different devices: /device:TPU:17 before, /device:TPU:9 now
where the time goes in v3:
time: 64.8 us; the launch traced here: 64.5 us
  Pallas kernels  63.9 us (99%)
    pallas_call x1, Pallas kernels, local(): pl.pallas_call(functools.partial(refine_kernel, n_a, n_r, capacity), out_...  57 us
    pallas_call x1, Pallas kernels, local(): pl.pallas_call(functools.partial(placed, angles), grid_spec=pltpu.Prefetc...  6.93 us

profile of v3, /device:TPU:9, one launch (start us, length us, event | category | flops | bytes accessed | tf_op | source)
XLA Modules:
  0.0 64.5 jit_solution(16835048386591322888)
XLA Ops:
  0.6 57.0 %refine.1 = (bf16[16,2,256,256]{3,2,1,0:T(8,128)(2,1)}, bf16[4,16,64,256]{3,2,1,0:T(8,128)(2,1)}, bf16[4,2,64,2048]{3,2,1,0:T(8,128)(2,1)}, s32[4,8,128]{2,1,0:T(8,128)}) custom-call(s32[12]{0:T(128)} %owner_ref.1, s32[12]{0:T(128)} %column_ref.1, s32[12]{0:T(128)} %angle_ref.1, bf16[2,256,256]{2,1,0:T(8,128)(2,1)} %probe.1, ...), custom_call_target="tpu_custom_call" | custom-call | tf_op jit(solution)/shard_map/refine/pallas_call | solution.py:326
  57.6 6.9 %place.1 = (bf16[8,1,64,2048]{3,2,1,0:T(8,128)(2,1)}, bf16[12,2,256,256]{3,2,1,0:T(8,128)(2,1)}) custom-call(s32[1]{0:T(128)} %bitcast.me_ref, s32[4,8,128]{2,1,0:T(8,128)} %get-tuple-element.8.refs_0_, bf16[4,2,64,2048]{3,2,1,0:T(8,128)(2,1)} %get-tuple-element.9.refs_1_, bf16[4,16,64,256]{3,2,1,0:T(8,128)(2,1)} %get-tuple-element.10.refs_2_, ...), custom_call_target="tpu_custom_call" | custom-call | tf_op jit(solution)/shard_map/place/pallas_call | solution.py:370
